TPU v7x, 32 devices: a whole 2x2x4 slice. The times are simulated.
32 devices in a mesh: groups: 2 (over x), dp: 16 (over z, y, core).
Axes of the slice: x: 2, y: 2, z: 4, core: 2. Of those that a mesh axis runs over, the one named last changes fastest.
Arguments:
- activations: bfloat16 [8192, 14336], P(('groups', 'dp')), parts along dimension 0, may hold values from -134 to 134
- out_grads: bfloat16 [8192, 4096], P(('groups', 'dp')), parts along dimension 0, may hold values from -45 to 45
- proj_in: bfloat16 [14336, 64], replicated, may hold values from -12 to 12
- proj_out: bfloat16 [4096, 64], replicated, may hold values from -12 to 12
- lengths: int32 [256], P(('groups', 'dp')), parts along dimension 0, may hold values from 1 to 32
- token_mask: int32 [8192], P(('groups', 'dp')), parts along dimension 0, may hold values 0 or 1
- query_ids: int32 [192], P(('groups', 'dp')), parts along dimension 0, may hold values from 0 to 7
- train_grads: bfloat16 [4096, 4096], P(('groups', 'dp')), parts along dimension 0, may hold values from -0.25 to 0.25
Outputs:
- influence: float32 [4096, 96], P(('groups', 'dp')), parts along dimension 0
There are 2 independent parts, one for each index of `groups`. A program takes and returns all parts, laid end to end along the dimension named above; an argument that names none is the same for every part. Nothing has to cross between parts.
All inputs are finite; a program needn't handle non-finite values. No bound on the sum of `token_mask` on one device may be relied on, other than what follows from the above.
Results may differ from a plain program's by a relative error of at most 0.0029.
Values may be sent and summed in bfloat16 or wider, within the bound.
A program may use at most 128 MiB of HBM per device.

v0:
```python
import jax
import jax.numpy as jnp
from jax import lax
from jax.sharding import PartitionSpec as P


def damp_factor(fisher):
    scale = jnp.trace(fisher) / fisher.shape[0] + 1e-06
    return jnp.linalg.cholesky(fisher / scale + 0.1 * jnp.eye(fisher.shape[0], dtype=fisher.dtype))


def condition_rows(chosen, chol_grad, chol_act):
    left = jax.vmap(lambda matrix: jax.scipy.linalg.cho_solve((chol_grad, True), matrix))(chosen)
    precond = jax.vmap(lambda matrix: jax.scipy.linalg.cho_solve((chol_act, True), matrix.T).T)(
        left
    )
    flat_rows = precond.reshape(precond.shape[0], -1)
    scaled = flat_rows / jnp.sqrt(jnp.mean(flat_rows * flat_rows, axis=1, keepdims=True) + 1e-06)
    return scaled.astype(jnp.bfloat16)


def score_rows(train_grads, rows):
    return lax.dot_general(
        train_grads, rows, (((1,), (1,)), ((), ())), preferred_element_type=jnp.float32
    )


def body(activations, out_grads, proj_in, proj_out, lengths, token_mask, query_ids, train_grads):
    act_proj = jnp.dot(activations, proj_in, preferred_element_type=jnp.float32)
    grad_proj = jnp.dot(out_grads, proj_out, preferred_element_type=jnp.float32)
    tokens_here = act_proj.shape[0]
    responses_here = lengths.shape[0]
    span = tokens_here // responses_here
    rank = act_proj.shape[1]
    valid = jnp.arange(span)[None, :] < lengths[:, None]
    weight = (valid.reshape(-1) & (token_mask == 1)).astype(jnp.float32)
    grad_weighted = grad_proj * weight[:, None]
    part_act = jnp.dot((act_proj * weight[:, None]).T, act_proj, precision=lax.Precision.HIGHEST)
    part_grad = jnp.dot(grad_weighted.T, grad_proj, precision=lax.Precision.HIGHEST)
    resp_grad = jnp.einsum(
        "rto,rti->roi",
        grad_weighted.reshape(responses_here, span, rank),
        act_proj.reshape(responses_here, span, rank),
        precision=lax.Precision.HIGHEST,
    )
    chosen = resp_grad[query_ids]
    fisher_act, fisher_grad = lax.psum((part_act, part_grad), "dp")
    chol_act = damp_factor(fisher_act)
    chol_grad = damp_factor(fisher_grad)
    query_rows = condition_rows(chosen, chol_grad, chol_act)
    return score_rows(train_grads, lax.all_gather(query_rows, "dp", axis=0, tiled=True))


def solution(mesh):
    in_specs = (
        P(("groups", "dp"), None),
        P(("groups", "dp"), None),
        P(),
        P(),
        P(("groups", "dp")),
        P(("groups", "dp")),
        P(("groups", "dp")),
        P(("groups", "dp"), None),
    )
    out_specs = P(("groups", "dp"), None)
    return jax.shard_map(body, mesh=mesh, in_specs=in_specs, out_specs=out_specs, check_vma=False)
```

profile of v0, /device:TPU:0, one launch (start us, length us, event | category | flops | bytes accessed | tf_op | source)
XLA Modules:
  0.0 128.8 jit_solution(622031373382457211)
XLA Ops:
  0.0 0.8 compare_select_fusion
  0.8 0.7 iota_compare_fusion.3
  1.6 0.7 and_convert_fusion
  2.3 6.0 %fusion.15 = f32[256,64]{0,1:T(8,128)S(1)} fusion(bf16[256,14336]{1,0:T(8,128)(2,1)} %param.11, bf16[14336,64]{0,1:T(8,128)(2,1)} %param.13), kind=kOutput, calls=%fused_computation.44 | convolution fusion | flops 469762048 | bytes 9240576 | tf_op jit(solution)/shard_map/dot_general | solution.py:29
  8.3 0.2 fusion.2
  8.7 0.8 broadcast_multiply_fusion
  9.4 0.2 fusion.14
  9.7 63.1 %all-reduce = (f32[64,64]{0,1:T(8,128)S(1)}, f32[64,64]{0,1:T(8,128)S(1)}) all-reduce(f32[64,64]{0,1:T(8,128)S(1)} %fusion.14, f32[64,64]{0,1:T(8,128)S(1)} %fusion.2), channel_id=1, replica_groups=mesh['groups'=2,'dp'=16] {'dp'}, use_global_device_ids=true, to_apply=%region_4.6 | all-reduce | flops 8192 | bytes 65536 | tf_op jit(solution)/shard_map/psum | solution.py:47
  72.7 0.6 select_reduce_fusion.3
  74.0 0.6 select_reduce_fusion.2
  75.4 5.8 %cholesky.55 = f32[64,64]{1,0:T(8,128)S(1)} custom-call(f32[64,64]{1,0:T(8,128)S(1)} %fusion.9), custom_call_target="Cholesky" | custom-call | tf_op jit(solution)/shard_map/jit(cholesky)/cholesky | solution.py:9
  81.2 0.6 compare_reduce_fusion
  81.9 0.7 fusion.6
  82.5 4.9 %custom-call.8 = f32[1,64,64]{1,2,0:T(8,128)S(1)} custom-call(f32[1,64,64]{2,1,0:T(8,128)S(1)} %fusion.6), custom_call_target="InvertDiagBlocksLowerTriangular" | custom-call | tf_op jit(solution)/shard_map/vmap(jit(_cho_solve))/triangular_solve | solution.py:13
  87.5 5.8 %cholesky.44 = f32[64,64]{1,0:T(8,128)S(1)} custom-call(f32[64,64]{1,0:T(8,128)S(1)} %fusion.12), custom_call_target="Cholesky" | custom-call | tf_op jit(solution)/shard_map/jit(cholesky)/cholesky | solution.py:9
  93.4 0.6 compare_reduce_fusion.1
  94.1 0.7 fusion.5
  94.7 4.9 %custom-call.9 = f32[1,64,64]{1,2,0:T(8,128)S(1)} custom-call(f32[1,64,64]{2,1,0:T(8,128)S(1)} %fusion.5), custom_call_target="InvertDiagBlocksLowerTriangular" | custom-call | tf_op jit(solution)/shard_map/vmap(jit(_cho_solve))/triangular_solve | solution.py:14
  99.7 0.6 fusion.16
  100.4 0.6 gather_fusion
  100.9 0.1 copy.36
  101.1 0.4 convolution_bitcast_fusion.3
  101.6 0.1 copy.37
  101.7 0.7 convolution_bitcast_fusion.1
  102.4 0.1 copy.39
  102.6 0.4 convolution_bitcast_fusion.2
  103.0 0.1 copy.40
  103.2 0.8 multiply_reduce_fusion
  104.0 0.1 copy.42
  104.3 20.8 %all-gather = bf16[16,6,4096]{2,1,0:T(8,128)(2,1)S(1)} all-gather(bf16[1,6,4096]{2,1,0:T(8,128)(2,1)S(1)} %fusion.4), channel_id=1, replica_groups=mesh['groups'=2,'dp'=16] {'dp'}, dimensions={0}, use_global_device_ids=true | all-gather | bytes 835584 | tf_op jit(solution)/shard_map/all_gather | solution.py:51
  125.1 1.1 reshape.52
  126.2 2.6 %convolution_bitcast_fusion.4 = f32[128,96]{0,1:T(8,128)} fusion(bf16[96,4096]{1,0:T(8,128)(2,1)} %reshape.52, bf16[128,4096]{1,0:T(8,128)(2,1)} %param.18), kind=kOutput, calls=%fused_computation.5 | convolution fusion | flops 100663296 | bytes 1884160 | tf_op jit(solution)/shard_map/dot_general | solution.py:23
  (22 shorter events, 0.9 us)
Async XLA Ops:
  0.0 8.7 %copy-start = (bf16[256,4096]{1,0:T(8,128)(2,1)S(1)}, bf16[256,4096]{1,0:T(8,128)(2,1)}, u32[]{:S(2)}) copy-start(bf16[256,4096]{1,0:T(8,128)(2,1)} %param.12) | copy-start | bytes 6291460
  2.3 6.4 %copy-start.1 = (bf16[4096,64]{0,1:T(8,128)(2,1)S(1)}, bf16[4096,64]{0,1:T(8,128)(2,1)}, u32[]{:S(2)}) copy-start(bf16[4096,64]{0,1:T(8,128)(2,1)} %param.14) | copy-start | bytes 1572868
where the time goes:
time: 129 us
  blocking collectives  83.9 us (65%)
  other arithmetic  27.7 us (21%)
  matrix products  12.7 us (10%)
  local copies, waits for them, and re-layouts  3 us (2%)
  between operations  1.53 us (1%)
    psum x1, blocking collectives, body(): fisher_act, fisher_grad = lax.psum((part_act, part_grad), 'dp')  63.1 us
    all_gather x1, blocking collectives, body(): lax.all_gather(query_rows, 'dp', axis=0, tiled=True)  20.8 us
    another operation x6, other arithmetic, damp_factor(): jnp.linalg.cholesky(fisher / scale + 0.1 * jnp.eye(fisher.shape[0], dtype...  13 us
    dot_general x1, matrix products, body(): act_proj = jnp.dot(activations, proj_in, preferred_element_type=jnp.float32)  6.01 us
    another operation x2, other arithmetic, condition_rows(): jax.scipy.linalg.cho_solve((chol_grad, True), matrix)  5.55 us
    another operation x2, other arithmetic, condition_rows(): jax.scipy.linalg.cho_solve((chol_act, True), matrix.T)  5.55 us

commit v1 on v0

v1 whole, which is shorter than its diff:
```python
import functools

import jax
import jax.numpy as jnp
from jax import lax
from jax.experimental import pallas as pl
from jax.experimental.pallas import tpu as pltpu
from jax.sharding import PartitionSpec as P

MESH = pl.DeviceIdType.MESH
HIGHEST = lax.Precision.HIGHEST
CHUNK = 2048
PANEL = 4


def dot_t(a, b, dims, **kw):
    return lax.dot_general(a, b, (dims, ((), ())), preferred_element_type=jnp.float32, **kw)


def invert_pair(matrix):
    rank, width = matrix.shape
    tiles = [matrix[8 * t : 8 * t + 8, :] for t in range(rank // 8)]
    lane = lax.broadcasted_iota(jnp.int32, (8, width), 1)
    sub = lax.broadcasted_iota(jnp.int32, (8, width), 0)
    first = lane < rank
    column = jnp.where(first, lane, lane - rank)
    for base in range(0, rank, PANEL):
        own, start = base // 8, base % 8
        spread = [
            [
                jnp.where(
                    first,
                    jnp.broadcast_to(tile[:, base + j : base + j + 1], (8, width)),
                    jnp.broadcast_to(tile[:, rank + base + j : rank + base + j + 1], (8, width)),
                )
                for tile in tiles
            ]
            for j in range(PANEL)
        ]
        for j in range(PANEL):
            at = start + j
            here = sub == at
            at_col = column == base + j
            inv = 1.0 / spread[j][own][at : at + 1, :]
            row = jnp.where(at_col[0:1, :], 1.0, tiles[own][at : at + 1, :]) * inv
            for t in range(len(tiles)):
                new = jnp.where(at_col, 0.0, tiles[t]) - spread[j][t] * row
                tiles[t] = jnp.where(here, row, new) if t == own else new
            for k in range(j + 1, PANEL):
                factor = spread[k][own][at : at + 1, :] * inv
                for t in range(len(tiles)):
                    new = spread[k][t] - spread[j][t] * factor
                    spread[k][t] = jnp.where(here, factor, new) if t == own else new
    return jnp.concatenate(tiles, axis=0)


def kernel(
    n, lengths, query_ids, mask, act_hbm, grad_hbm, pin_hbm, pout_hbm, train_hbm, out,
    act_v, grad_v, pin_v, pout_v, train_v, part, landed, sums, total, wide, rows,
    load_sem, rs_send, rs_recv, ex_send, ex_recv, ag_send, ag_recv, row_send, row_recv,
):
    me = lax.axis_index("dp")
    tokens, n_in = act_hbm.shape
    n_out = grad_hbm.shape[1]
    rank = pin_hbm.shape[1]
    width = 2 * rank
    owners = part.shape[0]
    span_rows = part.shape[1]
    rep = n // owners

    loads = []
    sem_at = 0
    plan = []
    for x_hbm, w_hbm, x_v, w_v, depth in (
        (act_hbm, pin_hbm, act_v, pin_v, n_in),
        (grad_hbm, pout_hbm, grad_v, pout_v, n_out),
    ):
        for c in range(depth // CHUNK):
            cols = slice(c * CHUNK, (c + 1) * CHUNK)
            copies = (
                pltpu.make_async_copy(w_hbm.at[cols, :], w_v.at[cols, :], load_sem.at[sem_at]),
                pltpu.make_async_copy(x_hbm.at[:, cols], x_v.at[:, cols], load_sem.at[sem_at + 1]),
            )
            sem_at += 2
            for copy in copies:
                copy.start()
            plan.append((copies, x_v, w_v, cols))
    train_copy = pltpu.make_async_copy(train_hbm, train_v, load_sem.at[sem_at])
    train_copy.start()

    barrier = pltpu.get_barrier_semaphore()

    def greet(k, _):
        pl.semaphore_signal(
            barrier, inc=1, device_id={"dp": lax.rem(me + k, n)}, device_id_type=MESH
        )
        return 0

    lax.fori_loop(1, n, greet, 0)

    accs = {}
    for copies, x_v, w_v, cols in plan:
        for copy in copies:
            copy.wait()
        term = jnp.dot(x_v[:, cols], w_v[cols, :], preferred_element_type=jnp.float32)
        accs[id(x_v)] = accs[id(x_v)] + term if id(x_v) in accs else term
    act_proj, grad_proj = accs[id(act_v)], accs[id(grad_v)]

    slot = lax.broadcasted_iota(jnp.int32, (1, tokens), 1)
    n_resp = lengths.shape[0]
    span = tokens // n_resp
    response = slot // span
    length = jnp.zeros((1, tokens), jnp.int32)
    for r in range(n_resp):
        length = jnp.where(response == r, lengths[r], length)
    weight = jnp.where((slot - response * span < length) & (mask[...] == 1), 1.0, 0.0)

    both = jnp.concatenate([act_proj, grad_proj], axis=1)
    both_t = both.T * weight
    fisher = jnp.dot(both_t, both, precision=HIGHEST, preferred_element_type=jnp.float32)
    lane = lax.broadcasted_iota(jnp.int32, (rank, width), 1)
    packed = jnp.where(lane < rank, fisher[:rank, :], fisher[rank:, :])
    for c in range(owners):
        part[c] = packed[c * span_rows : (c + 1) * span_rows, :]

    pl.semaphore_wait(barrier, n - 1)

    team = me // owners
    seat = me - team * owners

    def peer(k):
        return lax.rem(seat + k, owners)

    def rs_copy(k):
        to = peer(k)
        return pltpu.make_async_remote_copy(
            src_ref=part.at[to], dst_ref=landed.at[k],
            send_sem=rs_send.at[k], recv_sem=rs_recv.at[k],
            device_id={"dp": team * owners + to}, device_id_type=MESH,
        )

    def start_rs(k, _):
        rs_copy(k).start()
        return 0

    lax.fori_loop(1, owners, start_rs, 0)

    n_query = query_ids.shape[0]
    grad_t = both_t[rank:, :]
    picked = jnp.concatenate(
        [jnp.where(response == query_ids[q], grad_t, 0.0) for q in range(n_query)], axis=0
    )
    chosen = jnp.dot(picked, act_proj, precision=HIGHEST, preferred_element_type=jnp.float32)

    def wait_rs(k, acc):
        rs_copy(k).wait()
        return acc + landed[k]

    mine = lax.fori_loop(1, owners, wait_rs, part[seat])
    if rep > 1:
        sums[0] = mine

        def ex_copy(k):
            return pltpu.make_async_remote_copy(
                src_ref=sums.at[0], dst_ref=sums.at[k],
                send_sem=ex_send.at[k], recv_sem=ex_recv.at[k],
                device_id={"dp": lax.rem(me + k * owners, n)}, device_id_type=MESH,
            )

        def start_ex(k, _):
            ex_copy(k).start()
            return 0

        def wait_ex(k, acc):
            ex_copy(k).wait()
            return acc + sums[k]

        lax.fori_loop(1, rep, start_ex, 0)
        mine = lax.fori_loop(1, rep, wait_ex, mine)
    total[seat] = mine

    def ag_copy(k):
        return pltpu.make_async_remote_copy(
            src_ref=total.at[seat], dst_ref=total.at[seat],
            send_sem=ag_send.at[k], recv_sem=ag_recv.at[k],
            device_id={"dp": team * owners + peer(k)}, device_id_type=MESH,
        )

    def start_ag(k, _):
        ag_copy(k).start()
        return 0

    def wait_ag(k, _):
        ag_copy(k).wait()
        return 0

    lax.fori_loop(1, owners, start_ag, 0)
    lax.fori_loop(1, owners, wait_ag, 0)

    summed = jnp.concatenate([total[c] for c in range(owners)], axis=0)
    row_at = lax.broadcasted_iota(jnp.int32, (rank, width), 0)
    left = lane < rank
    diag = row_at == jnp.where(left, lane, lane - rank)
    on_diag = jnp.where(diag, summed, 0.0)
    trace_act = jnp.sum(jnp.where(left, on_diag, 0.0), axis=(0, 1), keepdims=True)
    trace_grad = jnp.sum(jnp.where(left, 0.0, on_diag), axis=(0, 1), keepdims=True)
    scale = jnp.where(left, trace_act, trace_grad) / rank + 1e-06
    inverse = invert_pair(summed / scale + jnp.where(diag, 0.1, 0.0))

    swapped = pltpu.roll(inverse, rank, 1)
    inv_act_twice = jnp.where(left, inverse, swapped)
    inv_grad = swapped[:, :rank]
    right_done = jnp.dot(chosen, inv_act_twice, precision=HIGHEST, preferred_element_type=jnp.float32)
    for q in range(8):
        if q < n_query:
            value = jnp.dot(
                inv_grad, right_done[q * rank : (q + 1) * rank, :],
                precision=HIGHEST, preferred_element_type=jnp.float32,
            )
        else:
            value = jnp.zeros((rank, width), jnp.float32)
        wide[pl.ds(q, rank, stride=8), :] = value
    left8 = left[:8, :]
    pieces = [
        jnp.where(left8, wide[16 * p : 16 * p + 8, :], wide[16 * p + 8 : 16 * p + 16, :])
        for p in range(rank // 2)
    ]
    squares = pieces[0] * pieces[0]
    for piece in pieces[1:]:
        squares = squares + piece * piece
    mean = jnp.sum(squares, axis=1, keepdims=True) / (rank * rank)
    root = jnp.sqrt(mean + 1e-06)
    half = rank // 4
    for p in range(half):
        tile = jnp.concatenate([pieces[p] / root, pieces[p + half] / root], axis=0)
        rows[me, :, width * p : width * (p + 1)] = tile.astype(jnp.bfloat16)

    fours = n // 4
    place = lax.rem(me, 4)
    far = me + 2 - 4 * (place // 2)
    near = me + 1 - 2 * lax.rem(me, 2)

    def line(k):
        return lax.rem(me + 4 * k, n)

    def back(k):
        return lax.rem(me + n - 4 * k, n)

    def send(block, to, k):
        return pltpu.make_async_remote_copy(
            src_ref=rows.at[block], dst_ref=rows.at[block],
            send_sem=row_send.at[k], recv_sem=row_recv.at[k],
            device_id={"dp": to}, device_id_type=MESH,
        )

    def along(k):
        return send(me, line(k), k)

    def to_far(k):
        return send(back(k), far, fours + k)

    def to_near(k):
        return send(back(k), near, 2 * fours + k)

    def to_near_far(k):
        return send(lax.rem(far + n - 4 * k, n), near, 3 * fours + k)

    def start_line(k, _):
        along(k).start()
        return 0

    def forward(k, _):
        @pl.when(k > 0)
        def _():
            along(k).wait_recv()

        to_far(k).start()
        to_near(k).start()
        return 0

    def forward_far(k, _):
        to_far(k).wait_recv()
        to_near_far(k).start()
        return 0

    def finish(k, _):
        @pl.when(k > 0)
        def _():
            along(k).wait_send()

        to_far(k).wait_send()
        to_near(k).wait()
        to_near_far(k).wait()
        return 0

    lax.fori_loop(1, fours, start_line, 0)
    lax.fori_loop(0, fours, forward, 0)
    lax.fori_loop(0, fours, forward_far, 0)
    lax.fori_loop(0, fours, finish, 0)

    train_copy.wait()
    cut = rows.shape[2]
    gathered = rows[...].reshape(n * 16, cut)
    low = dot_t(train_v[:, :cut], gathered, ((1,), (1,)))
    high = dot_t(train_v[:, cut:], gathered, ((1,), (1,)))
    at = lax.broadcasted_iota(jnp.int32, (n * 16, n * n_query), 0)
    want = lax.broadcasted_iota(jnp.int32, (n * 16, n * n_query), 1)
    want = want // n_query * 16 + lax.rem(want, n_query)
    out[...] = jnp.dot(
        low, jnp.where(at == want, 1.0, 0.0), precision=HIGHEST, preferred_element_type=jnp.float32
    ) + jnp.dot(
        high, jnp.where(at == want + 8, 1.0, 0.0), precision=HIGHEST, preferred_element_type=jnp.float32
    )


def body(n, activations, out_grads, proj_in, proj_out, lengths, token_mask, query_ids, train_grads):
    tokens, n_in = activations.shape
    n_out = out_grads.shape[1]
    rank = proj_in.shape[1]
    n_query = query_ids.shape[0]
    owners = min(n, 16)
    span_rows = rank // owners
    n_loads = 2 * (n_in // CHUNK + n_out // CHUNK) + 1
    smem = pl.BlockSpec(memory_space=pltpu.SMEM)
    vmem = pl.BlockSpec(memory_space=pltpu.VMEM)
    hbm = pl.BlockSpec(memory_space=pl.ANY)
    dma = pltpu.SemaphoreType.DMA
    flops = 2 * tokens * rank * (n_in + n_out) + 2 * train_grads.size * n * n_query
    return pl.pallas_call(
        functools.partial(kernel, n),
        out_shape=jax.ShapeDtypeStruct((train_grads.shape[0], n * n_query), jnp.float32),
        in_specs=[smem, smem, vmem, hbm, hbm, hbm, hbm, hbm],
        out_specs=vmem,
        scratch_shapes=[
            pltpu.VMEM(activations.shape, jnp.bfloat16),
            pltpu.VMEM(out_grads.shape, jnp.bfloat16),
            pltpu.VMEM(proj_in.shape, jnp.bfloat16),
            pltpu.VMEM(proj_out.shape, jnp.bfloat16),
            pltpu.VMEM(train_grads.shape, jnp.bfloat16),
            pltpu.VMEM((owners, span_rows, 2 * rank), jnp.float32),
            pltpu.VMEM((owners, span_rows, 2 * rank), jnp.float32),
            pltpu.VMEM((max(n // owners, 1), span_rows, 2 * rank), jnp.float32),
            pltpu.VMEM((owners, span_rows, 2 * rank), jnp.float32),
            pltpu.VMEM((rank * 8, 2 * rank), jnp.float32),
            pltpu.VMEM((n, 16, rank * rank // 2), jnp.bfloat16),
            dma((n_loads,)),
            dma((owners,)),
            dma((owners,)),
            dma((max(n // owners, 1),)),
            dma((max(n // owners, 1),)),
            dma((owners,)),
            dma((owners,)),
            dma((n,)),
            dma((n,)),
        ],
        compiler_params=pltpu.CompilerParams(
            collective_id=0, has_side_effects=True, vmem_limit_bytes=56 * 1024 * 1024
        ),
        cost_estimate=pl.CostEstimate(flops=flops, bytes_accessed=16_000_000, transcendentals=0),
    )(
        lengths, query_ids, token_mask.reshape(1, tokens),
        activations, out_grads, proj_in, proj_out, train_grads,
    )


def solution(mesh):
    in_specs = (
        P(("groups", "dp"), None),
        P(("groups", "dp"), None),
        P(),
        P(),
        P(("groups", "dp")),
        P(("groups", "dp")),
        P(("groups", "dp")),
        P(("groups", "dp"), None),
    )
    out_specs = P(("groups", "dp"), None)
    run = functools.partial(body, mesh.shape["dp"])
    return jax.shard_map(run, mesh=mesh, in_specs=in_specs, out_specs=out_specs, check_vma=False)
```

time: 129 us -> 45.5 us (0.35)
  blocking collectives: 83.9 us -> 0 us
  Pallas kernels: 0 us -> 36.8 us
  other arithmetic: 27.7 us -> 0 us
  matrix products: 12.7 us -> 0 us
  local copies, waits for them, and re-layouts: 3 us -> 8.46 us
  between operations: 1.53 us -> 0.01 us
    psum x1 -> x0, blocking collectives: 63.1 us -> none  [body(): fisher_act, fisher_grad = lax.psum((part_act, part_grad), 'dp')]
    pallas_call x0 -> x1, Pallas kernels: none -> 36.8 us  [body(): pl.pallas_call(functools.partial(kernel, n), out_shape=jax.ShapeDtypeStru...]
    another operation x10 -> x0, other arithmetic: 24.1 us -> none  [the longest x6 13 us: damp_factor(): jnp.linalg.cholesky(fisher / scale + 0.1 * jnp.eye(fisher.shape[0], dtype...]
    all_gather x1 -> x0, blocking collectives: 20.8 us -> none  [body(): lax.all_gather(query_rows, 'dp', axis=0, tiled=True)]
    dot_general x6 -> x0, matrix products: 10.4 us -> none  [the longest x1 6.01 us: body(): act_proj = jnp.dot(activations, proj_in, preferred_element_type=jnp.float32)]
    unnamed x5 -> x2, local copies, waits for them, and re-layouts: 1.15 us -> 6.91 us
    another operation x4 -> x0, matrix products: 2.31 us -> none  [the longest x2 1.2 us: condition_rows(): jax.scipy.linalg.cho_solve((chol_act, True), matrix.T)]
    pallas_call x0 -> x1, local copies, waits for them, and re-layouts: none -> 1.55 us  [body(): pl.pallas_call(functools.partial(kernel, n), out_shape=jax.ShapeDtypeStru...]
where the time goes in v1:
time: 45.5 us; the launch traced here: 45.3 us
  Pallas kernels  36.8 us (81%)
  local copies, waits for them, and re-layouts  8.46 us (19%)
    pallas_call x1, Pallas kernels, body(): pl.pallas_call(functools.partial(kernel, n), out_shape=jax.ShapeDtypeStru...  36.8 us
    unnamed x2, local copies, waits for them, and re-layouts  6.91 us
    pallas_call x1, local copies, waits for them, and re-layouts, body(): pl.pallas_call(functools.partial(kernel, n), out_shape=jax.ShapeDtypeStru...  1.55 us

profile of v1, /device:TPU:0, one launch (start us, length us, event | category | flops | bytes accessed | tf_op | source)
XLA Modules:
  0.0 45.3 jit_solution(9951252124655449197)
XLA Ops:
  0.0 2.3 %copy.10.pout_hbm = bf16[4096,64]{1,0:T(8,128)(2,1)} copy(bf16[4096,64]{0,1:T(8,128)(2,1)} %param.11) | data formatting | bytes 1048576 | tf_op args[3]
  2.3 4.6 %copy.9.pin_hbm = bf16[14336,64]{1,0:T(8,128)(2,1)} copy(bf16[14336,64]{0,1:T(8,128)(2,1)} %param.10) | data formatting | bytes 3670016 | tf_op args[2]
  6.9 36.8 %shard_map.82 = f32[128,96]{1,0:T(8,128)} custom-call(s32[8]{0:T(128)} %lengths.1, s32[6]{0:T(128)} %query_ids.1, s32[1,256]{1,0:T(1,128)} %bitcast.1, bf16[256,14336]{1,0:T(8,128)(2,1)} %act_hbm.1, bf16[256,4096]{1,0:T(8,128)(2,1)} %grad_hbm.1, bf16[14336,64]{1,0:T(8,128)(2,1)} %copy.9.pin_hbm, bf16[4096,64]{1,0:T(8,128)(2,1)} %copy.10.pout_hbm, ...), custom_call_target="tpu_custom_call" | custom-call | flops 704643072 | bytes 16000000 | tf_op jit(solution)/shard_map/pallas_call | solution.py:329
  43.7 1.6 %copy.11 = f32[128,96]{0,1:T(8,128)} copy(f32[128,96]{1,0:T(8,128)} %shard_map.82) | data formatting | bytes 98304 | tf_op jit(solution)/shard_map/pallas_call | solution.py:329

commit v2 on v1

--- a/solution.py
+++ b/solution.py
@@ -62,7 +62,7 @@
     me = lax.axis_index("dp")
     tokens, n_in = act_hbm.shape
     n_out = grad_hbm.shape[1]
-    rank = pin_hbm.shape[1]
+    rank = pin_hbm.shape[0]
     width = 2 * rank
     owners = part.shape[0]
     span_rows = part.shape[1]
@@ -78,7 +78,7 @@
         for c in range(depth // CHUNK):
             cols = slice(c * CHUNK, (c + 1) * CHUNK)
             copies = (
-                pltpu.make_async_copy(w_hbm.at[cols, :], w_v.at[cols, :], load_sem.at[sem_at]),
+                pltpu.make_async_copy(w_hbm.at[:, cols], w_v.at[:, cols], load_sem.at[sem_at]),
                 pltpu.make_async_copy(x_hbm.at[:, cols], x_v.at[:, cols], load_sem.at[sem_at + 1]),
             )
             sem_at += 2
@@ -102,7 +102,7 @@
     for copies, x_v, w_v, cols in plan:
         for copy in copies:
             copy.wait()
-        term = jnp.dot(x_v[:, cols], w_v[cols, :], preferred_element_type=jnp.float32)
+        term = dot_t(x_v[:, cols], w_v[:, cols], ((1,), (1,)))
         accs[id(x_v)] = accs[id(x_v)] + term if id(x_v) in accs else term
     act_proj, grad_proj = accs[id(act_v)], accs[id(grad_v)]
 
@@ -301,16 +301,12 @@
     train_copy.wait()
     cut = rows.shape[2]
     gathered = rows[...].reshape(n * 16, cut)
-    low = dot_t(train_v[:, :cut], gathered, ((1,), (1,)))
-    high = dot_t(train_v[:, cut:], gathered, ((1,), (1,)))
-    at = lax.broadcasted_iota(jnp.int32, (n * 16, n * n_query), 0)
-    want = lax.broadcasted_iota(jnp.int32, (n * 16, n * n_query), 1)
-    want = want // n_query * 16 + lax.rem(want, n_query)
-    out[...] = jnp.dot(
-        low, jnp.where(at == want, 1.0, 0.0), precision=HIGHEST, preferred_element_type=jnp.float32
-    ) + jnp.dot(
-        high, jnp.where(at == want + 8, 1.0, 0.0), precision=HIGHEST, preferred_element_type=jnp.float32
-    )
+    low = dot_t(gathered, train_v[:, :cut], ((1,), (1,)))
+    high = dot_t(gathered, train_v[:, cut:], ((1,), (1,)))
+    for d in range(n):
+        out[d * n_query : (d + 1) * n_query, :] = (
+            low[16 * d : 16 * d + n_query, :] + high[16 * d + 8 : 16 * d + 8 + n_query, :]
+        )
 
 
 def body(n, activations, out_grads, proj_in, proj_out, lengths, token_mask, query_ids, train_grads):
@@ -328,14 +324,14 @@
     flops = 2 * tokens * rank * (n_in + n_out) + 2 * train_grads.size * n * n_query
     return pl.pallas_call(
         functools.partial(kernel, n),
-        out_shape=jax.ShapeDtypeStruct((train_grads.shape[0], n * n_query), jnp.float32),
+        out_shape=jax.ShapeDtypeStruct((n * n_query, train_grads.shape[0]), jnp.float32),
         in_specs=[smem, smem, vmem, hbm, hbm, hbm, hbm, hbm],
         out_specs=vmem,
         scratch_shapes=[
             pltpu.VMEM(activations.shape, jnp.bfloat16),
             pltpu.VMEM(out_grads.shape, jnp.bfloat16),
-            pltpu.VMEM(proj_in.shape, jnp.bfloat16),
-            pltpu.VMEM(proj_out.shape, jnp.bfloat16),
+            pltpu.VMEM((rank, n_in), jnp.bfloat16),
+            pltpu.VMEM((rank, n_out), jnp.bfloat16),
             pltpu.VMEM(train_grads.shape, jnp.bfloat16),
             pltpu.VMEM((owners, span_rows, 2 * rank), jnp.float32),
             pltpu.VMEM((owners, span_rows, 2 * rank), jnp.float32),
@@ -359,8 +355,8 @@
         cost_estimate=pl.CostEstimate(flops=flops, bytes_accessed=16_000_000, transcendentals=0),
     )(
         lengths, query_ids, token_mask.reshape(1, tokens),
-        activations, out_grads, proj_in, proj_out, train_grads,
-    )
+        activations, out_grads, proj_in.T, proj_out.T, train_grads,
+    ).T
 
 
 def solution(mesh):

time: 45.5 us -> 39.7 us (0.87)
  local copies, waits for them, and re-layouts: 8.46 us -> 1.42 us
  Pallas kernels: 36.8 us -> 38.1 us
    unnamed x2 -> x1, local copies, waits for them, and re-layouts: 6.91 us -> 1.42 us
    pallas_call x1 -> x0, local copies, waits for them, and re-layouts: 1.55 us -> none  [body(): pl.pallas_call(functools.partial(kernel, n), out_shape=jax.ShapeDtypeStru...]
    pallas_call x1, Pallas kernels: 36.8 us -> 38.1 us  [body(): pl.pallas_call(functools.partial(kernel, n), out_shape=jax.ShapeDtypeStru...]
where the time goes in v2:
time: 39.7 us; the launch traced here: 39.5 us
  Pallas kernels  38.1 us (96%)
  local copies, waits for them, and re-layouts  1.42 us (4%)
    pallas_call x1, Pallas kernels, body(): pl.pallas_call(functools.partial(kernel, n), out_shape=jax.ShapeDtypeStru...  38.1 us
    unnamed x1, local copies, waits for them, and re-layouts  1.42 us

profile of v2, /device:TPU:0, one launch (start us, length us, event | category | flops | bytes accessed | tf_op | source)
XLA Modules:
  0.0 39.5 jit_solution(4519713787154652444)
XLA Ops:
  0.0 38.1 %shard_map.82 = f32[96,128]{1,0:T(8,128)} custom-call(s32[8]{0:T(128)} %lengths.1, s32[6]{0:T(128)} %query_ids.1, s32[1,256]{1,0:T(1,128)} %bitcast.7, bf16[256,14336]{1,0:T(8,128)(2,1)} %act_hbm.1, bf16[256,4096]{1,0:T(8,128)(2,1)} %grad_hbm.1, bf16[64,14336]{1,0:T(8,128)(2,1)} %bitcast.4, bf16[64,4096]{1,0:T(8,128)(2,1)} %bitcast.5, ...), custom_call_target="tpu_custom_call" | custom-call | flops 704643072 | bytes 16000000 | tf_op jit(solution)/shard_map/pallas_call | solution.py:325
  38.1 1.4 %copy.10 = f32[128,96]{0,1:T(8,128)} copy(f32[128,96]{0,1:T(8,128)} %bitcast.6) | data formatting | bytes 98304

commit v3 on v2

--- a/solution.py
+++ b/solution.py
@@ -68,7 +68,6 @@
     span_rows = part.shape[1]
     rep = n // owners
 
-    loads = []
     sem_at = 0
     plan = []
     for x_hbm, w_hbm, x_v, w_v, depth in (
@@ -90,13 +89,19 @@
 
     barrier = pltpu.get_barrier_semaphore()
 
-    def greet(k, _):
-        pl.semaphore_signal(
-            barrier, inc=1, device_id={"dp": lax.rem(me + k, n)}, device_id_type=MESH
-        )
-        return 0
-
-    lax.fori_loop(1, n, greet, 0)
+    chips = n // 2
+    core = lax.rem(me, 2)
+    near = me + 1 - 2 * core
+
+    def greet(to):
+        pl.semaphore_signal(barrier, inc=1, device_id={"dp": to}, device_id_type=MESH)
+
+    def greet_chip(k, _):
+        greet(lax.rem(me + 2 * k, n))
+        return 0
+
+    greet(near)
+    lax.fori_loop(1, chips, greet_chip, 0)
 
     accs = {}
     for copies, x_v, w_v, cols in plan:
@@ -123,7 +128,7 @@
     for c in range(owners):
         part[c] = packed[c * span_rows : (c + 1) * span_rows, :]
 
-    pl.semaphore_wait(barrier, n - 1)
+    pl.semaphore_wait(barrier, chips)
 
     team = me // owners
     seat = me - team * owners
@@ -230,21 +235,21 @@
         squares = squares + piece * piece
     mean = jnp.sum(squares, axis=1, keepdims=True) / (rank * rank)
     root = jnp.sqrt(mean + 1e-06)
-    half = rank // 4
+    pieces = [piece / root for piece in pieces]
+    sub8 = row_at[:8, :]
+    body_count = rank // 2 * n_query // 8
+    tail_count = rank // 2 - body_count
+    third = n_query // 2
+    packed_rows = []
+    for p in range(body_count):
+        tail, q = pieces[body_count + p % tail_count], p // tail_count
+        last = jnp.where(sub8 == 6, tail[q : q + 1, :], tail[third + q : third + q + 1, :])
+        packed_rows.append(jnp.where(sub8 < 6, pieces[p], last))
+    half = body_count // 2
+    mine_at = core * chips + me // 2
     for p in range(half):
-        tile = jnp.concatenate([pieces[p] / root, pieces[p + half] / root], axis=0)
-        rows[me, :, width * p : width * (p + 1)] = tile.astype(jnp.bfloat16)
-
-    fours = n // 4
-    place = lax.rem(me, 4)
-    far = me + 2 - 4 * (place // 2)
-    near = me + 1 - 2 * lax.rem(me, 2)
-
-    def line(k):
-        return lax.rem(me + 4 * k, n)
-
-    def back(k):
-        return lax.rem(me + n - 4 * k, n)
+        tile = jnp.concatenate([packed_rows[p], packed_rows[p + half]], axis=0)
+        rows[mine_at, :, width * p : width * (p + 1)] = tile.astype(jnp.bfloat16)
 
     def send(block, to, k):
         return pltpu.make_async_remote_copy(
@@ -253,59 +258,58 @@
             device_id={"dp": to}, device_id_type=MESH,
         )
 
-    def along(k):
-        return send(me, line(k), k)
-
-    def to_far(k):
-        return send(back(k), far, fours + k)
+    def to_chip(k):
+        return send(mine_at, lax.rem(me + 2 * k, n), k)
 
     def to_near(k):
-        return send(back(k), near, 2 * fours + k)
-
-    def to_near_far(k):
-        return send(lax.rem(far + n - 4 * k, n), near, 3 * fours + k)
-
-    def start_line(k, _):
-        along(k).start()
-        return 0
-
-    def forward(k, _):
-        @pl.when(k > 0)
-        def _():
-            along(k).wait_recv()
-
-        to_far(k).start()
+        return send(core * chips + lax.rem(me // 2 + chips - k, chips), near, chips + k)
+
+    def start_chip(k, _):
+        to_chip(k).start()
+        return 0
+
+    def hand_on(k, _):
+        to_chip(k).wait_recv()
         to_near(k).start()
         return 0
 
-    def forward_far(k, _):
-        to_far(k).wait_recv()
-        to_near_far(k).start()
-        return 0
-
     def finish(k, _):
-        @pl.when(k > 0)
-        def _():
-            along(k).wait_send()
-
-        to_far(k).wait_send()
         to_near(k).wait()
-        to_near_far(k).wait()
-        return 0
-
-    lax.fori_loop(1, fours, start_line, 0)
-    lax.fori_loop(0, fours, forward, 0)
-    lax.fori_loop(0, fours, forward_far, 0)
-    lax.fori_loop(0, fours, finish, 0)
+        to_chip(k).wait_send()
+        return 0
+
+    lax.fori_loop(1, chips, start_chip, 0)
+    to_near(0).start()
+    lax.fori_loop(1, chips, hand_on, 0)
+    lax.fori_loop(1, chips, finish, 0)
+    to_near(0).wait()
 
     train_copy.wait()
     cut = rows.shape[2]
     gathered = rows[...].reshape(n * 16, cut)
-    low = dot_t(gathered, train_v[:, :cut], ((1,), (1,)))
-    high = dot_t(gathered, train_v[:, cut:], ((1,), (1,)))
+    ends = 2 * cut
+    tail = train_v.shape[1] - ends
+    over = cut - tail
+
+    def score(row_cols, train_cols):
+        return dot_t(gathered[:, row_cols], train_v[:, train_cols], ((1,), (1,)))
+
+    low = score(slice(0, cut), slice(0, cut))
+    high = score(slice(0, cut), slice(cut, ends))
+    tail_a = score(slice(0, tail), slice(ends, ends + tail))
+    tail_b_low = score(slice(tail, cut), slice(ends, ends + over))
+    tail_b_high = score(slice(0, tail - over), slice(ends + over, ends + tail))
+    tail_c = score(slice(tail - over, cut), slice(ends, ends + tail))
     for d in range(n):
+        at = 16 * (d % 2 * chips + d // 2)
+        last = []
+        for r in (6, 7):
+            lo, hi = slice(at + r, at + r + 1), slice(at + 8 + r, at + 9 + r)
+            last += [tail_a[lo, :], tail_b_low[lo, :] + tail_b_high[hi, :], tail_c[hi, :]]
         out[d * n_query : (d + 1) * n_query, :] = (
-            low[16 * d : 16 * d + n_query, :] + high[16 * d + 8 : 16 * d + 8 + n_query, :]
+            low[at : at + n_query, :]
+            + high[at + 8 : at + 8 + n_query, :]
+            + jnp.concatenate(last, axis=0)
         )
 
 
@@ -314,7 +318,7 @@
     n_out = out_grads.shape[1]
     rank = proj_in.shape[1]
     n_query = query_ids.shape[0]
-    owners = min(n, 16)
+    owners = 2
     span_rows = rank // owners
     n_loads = 2 * (n_in // CHUNK + n_out // CHUNK) + 1
     smem = pl.BlockSpec(memory_space=pltpu.SMEM)
@@ -338,7 +342,7 @@
             pltpu.VMEM((max(n // owners, 1), span_rows, 2 * rank), jnp.float32),
             pltpu.VMEM((owners, span_rows, 2 * rank), jnp.float32),
             pltpu.VMEM((rank * 8, 2 * rank), jnp.float32),
-            pltpu.VMEM((n, 16, rank * rank // 2), jnp.bfloat16),
+            pltpu.VMEM((n, 16, rank * rank * n_query // 16), jnp.bfloat16),
             dma((n_loads,)),
             dma((owners,)),
             dma((owners,)),

time: 39.7 us -> 36.3 us (0.914); the launches traced: 39.5 us -> 35.7 us
  Pallas kernels: 38.1 us -> 34.2 us
    pallas_call x1, Pallas kernels: 38.1 us -> 34.2 us  [body(): pl.pallas_call(functools.partial(kernel, n), out_shape=jax.ShapeDtypeStru...]
where the time goes in v3:
time: 36.3 us; the launch traced here: 35.7 us
  Pallas kernels  34.2 us (94%)
  local copies, waits for them, and re-layouts  1.42 us (4%)
    pallas_call x1, Pallas kernels, body(): pl.pallas_call(functools.partial(kernel, n), out_shape=jax.ShapeDtypeStru...  34.2 us
    unnamed x1, local copies, waits for them, and re-layouts  1.42 us

profile of v3, /device:TPU:0, one launch (start us, length us, event | category | flops | bytes accessed | tf_op | source)
XLA Modules:
  0.0 35.7 jit_solution(16358815938735811102)
XLA Ops:
  0.0 34.2 %shard_map.82 = f32[96,128]{1,0:T(8,128)} custom-call(s32[8]{0:T(128)} %lengths.1, s32[6]{0:T(128)} %query_ids.1, s32[1,256]{1,0:T(1,128)} %bitcast.7, bf16[256,14336]{1,0:T(8,128)(2,1)} %act_hbm.1, bf16[256,4096]{1,0:T(8,128)(2,1)} %grad_hbm.1, bf16[64,14336]{1,0:T(8,128)(2,1)} %bitcast.4, bf16[64,4096]{1,0:T(8,128)(2,1)} %bitcast.5, ...), custom_call_target="tpu_custom_call" | custom-call | flops 704643072 | bytes 16000000 | tf_op jit(solution)/shard_map/pallas_call | solution.py:329
  34.2 1.4 %copy.10 = f32[128,96]{0,1:T(8,128)} copy(f32[128,96]{0,1:T(8,128)} %bitcast.6) | data formatting | bytes 98304

commit v4 on v3

--- a/solution.py
+++ b/solution.py
@@ -68,6 +68,22 @@
     span_rows = part.shape[1]
     rep = n // owners
 
+    barrier = pltpu.get_barrier_semaphore()
+
+    chips = n // 2
+    core = lax.rem(me, 2)
+    near = me + 1 - 2 * core
+
+    def greet(to):
+        pl.semaphore_signal(barrier, inc=1, device_id={"dp": to}, device_id_type=MESH)
+
+    def greet_chip(k, _):
+        greet(lax.rem(me + 2 * k, n))
+        return 0
+
+    greet(near)
+    lax.fori_loop(1, chips, greet_chip, 0)
+
     sem_at = 0
     plan = []
     for x_hbm, w_hbm, x_v, w_v, depth in (
@@ -87,27 +103,12 @@
     train_copy = pltpu.make_async_copy(train_hbm, train_v, load_sem.at[sem_at])
     train_copy.start()
 
-    barrier = pltpu.get_barrier_semaphore()
-
-    chips = n // 2
-    core = lax.rem(me, 2)
-    near = me + 1 - 2 * core
-
-    def greet(to):
-        pl.semaphore_signal(barrier, inc=1, device_id={"dp": to}, device_id_type=MESH)
-
-    def greet_chip(k, _):
-        greet(lax.rem(me + 2 * k, n))
-        return 0
-
-    greet(near)
-    lax.fori_loop(1, chips, greet_chip, 0)
-
     accs = {}
     for copies, x_v, w_v, cols in plan:
         for copy in copies:
             copy.wait()
-        term = dot_t(x_v[:, cols], w_v[:, cols], ((1,), (1,)))
+        upright = w_v[:, cols].astype(jnp.float32).T.astype(jnp.bfloat16)
+        term = jnp.dot(x_v[:, cols], upright, preferred_element_type=jnp.float32)
         accs[id(x_v)] = accs[id(x_v)] + term if id(x_v) in accs else term
     act_proj, grad_proj = accs[id(act_v)], accs[id(grad_v)]
 

time: 36.3 us -> 35.3 us (0.972)
  Pallas kernels: 34.2 us -> 33.3 us
    pallas_call x1, Pallas kernels: 34.2 us -> 33.3 us  [body(): pl.pallas_call(functools.partial(kernel, n), out_shape=jax.ShapeDtypeStru...]
where the time goes in v4:
time: 35.3 us; the launch traced here: 34.7 us
  Pallas kernels  33.3 us (94%)
  local copies, waits for them, and re-layouts  1.42 us (4%)
    pallas_call x1, Pallas kernels, body(): pl.pallas_call(functools.partial(kernel, n), out_shape=jax.ShapeDtypeStru...  33.3 us
    unnamed x1, local copies, waits for them, and re-layouts  1.42 us

profile of v4, /device:TPU:0, one launch (start us, length us, event | category | flops | bytes accessed | tf_op | source)
XLA Modules:
  0.0 34.7 jit_solution(5920173223415653422)
XLA Ops:
  0.0 33.3 %shard_map.82 = f32[96,128]{1,0:T(8,128)} custom-call(s32[8]{0:T(128)} %lengths.1, s32[6]{0:T(128)} %query_ids.1, s32[1,256]{1,0:T(1,128)} %bitcast.7, bf16[256,14336]{1,0:T(8,128)(2,1)} %act_hbm.1, bf16[256,4096]{1,0:T(8,128)(2,1)} %grad_hbm.1, bf16[64,14336]{1,0:T(8,128)(2,1)} %bitcast.4, bf16[64,4096]{1,0:T(8,128)(2,1)} %bitcast.5, ...), custom_call_target="tpu_custom_call" | custom-call | flops 704643072 | bytes 16000000 | tf_op jit(solution)/shard_map/pallas_call | solution.py:330
  33.3 1.4 %copy.10 = f32[128,96]{0,1:T(8,128)} copy(f32[128,96]{0,1:T(8,128)} %bitcast.6) | data formatting | bytes 98304
